TPU v7x, 32 devices: a whole 2x2x4 slice. The times are simulated.
32 devices in a mesh: seq: 16 (over z, y, core), fsdp: 2 (over x).
Axes of the slice: x: 2, y: 2, z: 4, core: 2. Of those that a mesh axis runs over, the one named last changes fastest.
Arguments:
- inputs: bfloat16 [4, 4096, 1536], P('fsdp', 'seq'), may hold values from -6 to 6
- gain: float32 [1536], replicated, may hold values from 0.1 to 1.9
- param: bfloat16 [1536, 3, 1536], P('fsdp'), may hold values from -6 to 6
- cotangent: bfloat16 [4, 4096, 1536], P('fsdp', 'seq'), may hold values from -12 to 12
- noise: bfloat16 [1536, 3, 1536], P('fsdp'), may hold values from -6 to 6
Outputs:
- outputs: bfloat16 [4, 4096, 1536], P('fsdp', 'seq')
- new_param: bfloat16 [1536, 3, 1536], P('fsdp')
All inputs are finite; a program needn't handle non-finite values.
Results may differ from a plain program's by a relative error of at most 0.012.
Values may be sent and summed in bfloat16 or wider, within the bound.
A program may use at most 128 MiB of HBM per device.

v0:
```python
import math

import jax
import jax.numpy as jnp
from jax import lax
from jax.sharding import PartitionSpec as P

DILATION_STEP = 16


def padded(x, sides, width):
    for axis, dim in sides:
        count, length = (lax.axis_size(axis), x.shape[dim])
        up = [(i, (i + 1) % count) for i in range(count - 1)]
        down = [(j, i) for i, j in up]
        last = lax.slice_in_dim(x, length - width, length, axis=dim)
        first = lax.slice_in_dim(x, 0, width, axis=dim)
        before = lax.ppermute(last, axis, up)
        after = lax.ppermute(first, axis, down)
        x = jnp.concatenate([before, x, after], axis=dim)
    return x


def normalise(values, gain):
    floats = values.astype(jnp.float32)
    factor = lax.rsqrt(jnp.mean(floats * floats, axis=-1, keepdims=True) + 1e-06)
    return jax.nn.gelu(floats * factor * gain).astype(jnp.bfloat16)


def convolve(source_rows, kernel, scale):
    span_length = source_rows.shape[1] - 2 * DILATION_STEP
    total = jnp.zeros((source_rows.shape[0], span_length, kernel.shape[0]), jnp.float32)
    for kernel_tap in range(3):
        input_window = source_rows[
            :, kernel_tap * DILATION_STEP : kernel_tap * DILATION_STEP + span_length, :
        ]
        total = total + lax.dot_general(
            input_window,
            kernel[:, kernel_tap, :],
            (((2,), (1,)), ((), ())),
            preferred_element_type=jnp.float32,
        )
    return total * scale


def shards(inputs, gain, param, cotangent, noise):
    seqs, span_length, width = inputs.shape
    scale = 1.0 / math.sqrt(3.0 * width)
    total_rows = seqs * lax.axis_size("fsdp") * span_length * lax.axis_size("seq")
    eta = math.sqrt(3.0 * width / total_rows)
    hidden_state = normalise(inputs, gain)
    padded_input = padded(hidden_state, (("seq", 1),), DILATION_STEP)
    mixed = convolve(padded_input, lax.all_gather(param, "fsdp", axis=0, tiled=True), scale)
    taps = []
    for kernel_tap in range(3):
        input_window = padded_input[
            :, kernel_tap * DILATION_STEP : kernel_tap * DILATION_STEP + span_length, :
        ]
        taps.append(
            lax.dot_general(
                cotangent,
                input_window,
                (((0, 1), (0, 1)), ((), ())),
                preferred_element_type=jnp.float32,
            )
        )
    term = (jnp.stack(taps, axis=1) * scale).astype(jnp.bfloat16)
    term = lax.optimization_barrier(term)
    share = lax.psum_scatter(
        term.astype(jnp.float32).astype(jnp.bfloat16), "fsdp", scatter_dimension=0, tiled=True
    ).astype(jnp.float32)
    seq_share = lax.psum_scatter(share, "seq", scatter_dimension=0, tiled=True)
    piece_rows = seq_share.shape[0]
    offset = lax.axis_index("seq") * piece_rows
    own_param = lax.dynamic_slice_in_dim(param, offset, piece_rows, 0)
    own_noise = lax.dynamic_slice_in_dim(noise, offset, piece_rows, 0)
    updated = (
        own_param.astype(jnp.float32)
        - eta * seq_share
        + math.sqrt(2.0 * eta) * own_noise.astype(jnp.float32)
    )
    new_param = lax.all_gather(updated.astype(jnp.bfloat16), "seq", axis=0, tiled=True)
    outputs = (inputs.astype(jnp.float32) + mixed).astype(jnp.bfloat16)
    return (outputs, new_param)


def solution(mesh):
    placed = (
        P("fsdp", "seq", None),
        P(),
        P("fsdp", None, None),
        P("fsdp", "seq", None),
        P("fsdp", None, None),
    )
    return jax.shard_map(
        shards,
        mesh=mesh,
        in_specs=placed,
        out_specs=(P("fsdp", "seq", None), P("fsdp", None, None)),
        check_vma=False,
    )
```

profile of v0, /device:TPU:0, one launch (start us, length us, event | category | flops | bytes accessed | tf_op | source)
XLA Modules:
  0.0 796.7 jit_solution(2017541967676426286)
XLA Ops:
  7.2 0.0 copy-start
  7.2 0.0 reduce-scatter.2.cloned.1.call-start
  7.2 1.9 fusion.7
  9.1 2.8 fusion.11
  11.9 1.3 collective-permute-start.1
  13.2 3.0 collective-permute-start
  16.3 2.6 convolution_bitcast_fusion.1
  19.0 0.0 collective-permute-done.1
  19.0 2.6 convolution_bitcast_fusion
  21.6 2.6 convolution_bitcast_fusion.2
  24.3 7.3 fusion
  31.6 0.0 reduce-scatter.2.cloned.1.call-update
  31.6 0.0 all-reduce.3.cloned.1.call-start
  31.7 164.8 %reduce-scatter.2.cloned.1.call-done = bf16[768,3,1536]{0,2,1:T(8,128)(2,1)} async-done(((bf16[1536,3,1536]{0,2,1:T(8,128)(2,1)}), bf16[768,3,1536]{0,2,1:T(8,128)(2,1)}) %reduce-scatter.2.cloned.1.call-update) | async-done | bytes 7077904 | tf_op jit(solution)/shard_map/reduce_scatter | solution.py:69
  196.5 17.1 %copy.23 = f32[768,3,1536]{2,1,0:T(4,128)} copy(bf16[768,3,1536]{0,2,1:T(8,128)(2,1)} %reduce-scatter.2.cloned.1.call-done) | data formatting | bytes 21233664 | tf_op jit(solution)/shard_map/convert_element_type | solution.py:71
  213.6 0.0 all-reduce.3.cloned.1.call-update
  213.6 0.0 copy-start.4
  213.6 0.0 all-gather.3.cloned.1.call-start
  213.6 0.7 all-gather.3.cloned.1.call-update
  214.3 0.2 all-gather.5.cloned.1.call-start
  214.6 0.6 dynamic-slice
  215.8 327.0 %all-reduce.3.cloned.1.call-done = f32[768,3,1536]{2,1,0:T(4,128)} async-done(((f32[768,3,1536]{2,1,0:T(4,128)}), f32[768,3,1536]{2,1,0:T(4,128)}) %all-reduce.3.cloned.1.call-update) | async-done | bytes 14155792
  542.9 1.5 constant_dynamic-slice_fusion
  544.3 2.3 fusion.20
  546.6 0.0 all-gather.5.cloned.1.call-update
  546.7 167.3 %all-gather.3.cloned.1.call-done = bf16[1536,3,1536]{2,0,1:T(8,128)(2,1)} async-done(((bf16[768,3,1536]{2,0,1:T(8,128)(2,1)}), bf16[1536,3,1536]{2,0,1:T(8,128)(2,1)}) %all-gather.3.cloned.1.call-update) | async-done | bytes 14155792 | tf_op jit(solution)/shard_map/all_gather | solution.py:53
  714.0 4.7 fusion.1
  718.6 1.8 copy-done.3
  720.4 2.6 fusion.2
  723.0 3.9 fusion.16
  726.9 56.7 %all-gather.5.cloned.1.call-done = bf16[768,3,1536]{2,0,1:T(8,128)(2,1)} async-done(((bf16[48,3,1536]{2,0,1:T(8,128)(2,1)}), bf16[768,3,1536]{2,0,1:T(8,128)(2,1)}) %all-gather.5.cloned.1.call-update) | async-done | bytes 7077904 | tf_op jit(solution)/shard_map/all_gather | solution.py:82
  783.6 6.5 copy.37
  (10 shorter events, 0.0 us)
Async XLA Ops:
  7.2 9.1 %copy-start = (bf16[2,256,1536]{2,1,0:T(8,128)(2,1)S(1)}, bf16[2,256,1536]{2,1,0:T(8,128)(2,1)}, u32[]{:S(2)}) copy-start(bf16[2,256,1536]{2,1,0:T(8,128)(2,1)} %param.8) | copy-start | bytes 4718596
  7.2 189.3 %reduce-scatter.2.cloned.1.call-start = ((), (), s32[]{:S(2)}) async-start(), calls=%async_computation.2 | async-start | bytes 21233664 | tf_op jit(solution)/shard_map/reduce_scatter | solution.py:69
  11.9 7.0 collective-permute-start.1
  13.2 8.4 %collective-permute-start = (bf16[2,16,1536]{2,1,0:T(8,128)(2,1)S(1)}, bf16[2,16,1536]{2,1,0:T(8,128)(2,1)S(1)}, u32[]{:S(2)}, u32[]{:S(2)}) collective-permute-start(bf16[2,16,1536]{2,1,0:T(8,128)(2,1)S(1)} %get-tuple-element.4), channel_id=1, source_target_pairs={{0,2},{2,4},{4,6},{6,8},{8,10},{10,12},{12,14},{14,16},{16,18},{18... | collective-permute-start | bytes 294920 | tf_op jit(solution)/shard_map/ppermute | solution.py:18
  31.6 511.2 %all-reduce.3.cloned.1.call-start = ((), (), s32[]{:S(2)}) async-start(), calls=%async_computation.4 | async-start | bytes 37748736
  213.6 1.0 copy-start.4
  213.6 500.4 %all-gather.3.cloned.1.call-start = ((), (), s32[]{:S(2)}) async-start(), calls=%async_computation.1 | async-start | bytes 21233664 | tf_op jit(solution)/shard_map/all_gather | solution.py:53
  214.3 569.3 %all-gather.5.cloned.1.call-start = ((), (), s32[]{:S(2)}) async-start(), calls=%async_computation.3 | async-start | bytes 7520256 | tf_op jit(solution)/shard_map/all_gather | solution.py:82
  714.0 6.4 copy-start.3
  720.4 2.6 copy-start.2
  783.6 6.5 copy-start.1
Sparse Core Ops, SparseCore 0:
  31.8 164.6 reduce-scatter.1
  213.7 329.1 all-reduce.2
  544.5 169.4 all-gather.2
  716.9 66.6 all-gather.4
where the time goes:
time: 797 us
  waiting for transfers between devices  717 us (90%)
  local copies, waits for them, and re-layouts  27.5 us (3%)
  matrix products  19.1 us (2%)
  between operations  14.5 us (2%)
  other arithmetic  14.3 us (2%)
    unnamed x5, waiting for transfers between devices  328 us
    all_gather x1, waiting for transfers between devices, shards(): lax.all_gather(param, 'fsdp', axis=0, tiled=True)  167 us
    reduce_scatter x1, waiting for transfers between devices, shards(): lax.psum_scatter(term.astype(jnp.float32).astype(jnp.bfloat16), 'fsdp', s...  165 us
    all_gather x1, waiting for transfers between devices, shards(): lax.all_gather(updated.astype(jnp.bfloat16), 'seq', axis=0, tiled=True)  56.7 us
    convert_element_type x1, local copies, waits for them, and re-layouts, shards(): share = lax.psum_scatter(term.astype(jnp.float32).astype(jnp.bfloat16), '...  17.1 us
  transfers between devices with their start and end apart: 6, of which 4 were waited for; matrix products, arithmetic and copies ran while one was open for 3% of the time, Pallas kernels for 0%

commit v1 on v0

--- a/solution.py
+++ b/solution.py
@@ -1,11 +1,17 @@
+import functools
 import math
 
 import jax
 import jax.numpy as jnp
 from jax import lax
+from jax.experimental import pallas as pl
+from jax.experimental.pallas import tpu as pltpu
 from jax.sharding import PartitionSpec as P
 
 DILATION_STEP = 16
+MESH = pl.DeviceIdType.MESH
+F32 = jnp.float32
+BF16 = jnp.bfloat16
 
 
 def padded(x, sides, width):
@@ -84,6 +90,334 @@
     return (outputs, new_param)
 
 
+def ring_kernel(
+    ring,
+    scale,
+    eta,
+    hidden,
+    cot,
+    inputs,
+    param_hbm,
+    noise_hbm,
+    outputs,
+    new_param,
+    param,
+    noise,
+    far_hidden,
+    far_cot,
+    own,
+    sib_out,
+    sib_in,
+    first,
+    part,
+    fresh,
+    mix_out,
+    mix_in,
+    load_sem,
+    hid_sem,
+    cot_sem,
+    sib_sem,
+    part_sem,
+    gather_sem,
+    share_sem,
+    mix_sem,
+):
+    seqs, span = inputs.shape[0], inputs.shape[1]
+    width, outs = inputs.shape[2], param.shape[1]
+    half = width // 2
+    rows = outs // ring
+    mine = rows // 2
+    depth = ring // 2
+    seq, fs = lax.axis_index("seq"), lax.axis_index("fsdp")
+    core, y, z = seq % 2, (seq // 2) % 2, seq // 4
+    p = z * (1 - y) + (ring - 1 - z) * y
+
+    def device(position):
+        low = jnp.where(position < depth, 0, 1)
+        zz = jnp.where(position < depth, position, ring - 1 - position)
+        return {"seq": (zz * 2 + low) * 2 + core}
+
+    right, left = device((p + 1) % ring), device((p + ring - 1) % ring)
+    sibling = {"seq": seq + 1 - 2 * core}
+    far = {"fsdp": 1 - fs}
+
+    param_load = pltpu.make_async_copy(param_hbm, param, load_sem.at[0])
+    own_rows = p * rows + core * mine
+    noise_load = pltpu.make_async_copy(
+        noise_hbm.at[:, pl.ds(own_rows, mine), :], noise, load_sem.at[1]
+    )
+    param_load.start()
+    noise_load.start()
+
+    barrier = pltpu.get_barrier_semaphore()
+    for other in (right, left, sibling, far):
+        pl.semaphore_signal(barrier, inc=1, device_id=other, device_id_type=MESH)
+    pl.semaphore_wait(barrier, 4)
+
+    def remote(src, dst, sems, index, to):
+        return pltpu.make_async_remote_copy(
+            src_ref=src,
+            dst_ref=dst,
+            send_sem=sems.at[(0,) + index],
+            recv_sem=sems.at[(1,) + index],
+            device_id=to,
+            device_id_type=MESH,
+        )
+
+    def chunk(j):
+        m = j // 2 + 1
+        offset = jnp.where(j % 2 == 0, ring - m, m)
+        return (p + jnp.where(j == ring - 1, 0, offset)) % ring
+
+    hid_copy = remote(hidden, far_hidden, hid_sem, (0,), far)
+    hid_copy.start()
+
+    def cot_copy(j):
+        q = chunk(j)
+        return remote(
+            cot.at[pl.ds((1 - fs) * outs + q * rows, rows), :],
+            far_cot.at[pl.ds(q * rows, rows), :],
+            cot_sem,
+            (j,),
+            far,
+        )
+
+    for j in range(ring):
+        cot_copy(j).start()
+
+    def forward(source, emit):
+        tile = 256
+        tiles = outs // tile
+
+        def body(i, carry):
+            b, o = i // tiles, pl.multiple_of((i % tiles) * tile, tile)
+            total = jnp.zeros((span, tile), F32)
+            for tap in range(3):
+                total += lax.dot_general(
+                    source[b, tap * DILATION_STEP : tap * DILATION_STEP + span, :],
+                    param[tap, pl.ds(o, tile), :],
+                    (((1,), (1,)), ((), ())),
+                    preferred_element_type=F32,
+                )
+            emit(b, o, tile, total * scale)
+            return carry
+
+        lax.fori_loop(0, seqs * tiles, body, 0)
+
+    def emit_near(b, o, tile, value):
+        at = pl.ds(pl.multiple_of(fs * outs + o, 128), tile)
+        outputs[b, :, at] = (inputs[b, :, at].astype(F32) + value).astype(BF16)
+
+    def emit_far(b, o, tile, value):
+        mix_out[b, :, pl.ds(o, tile)] = value.astype(BF16)
+
+    param_load.wait()
+    forward(hidden, emit_near)
+    hid_copy.wait_recv()
+
+    def sib_copy(j):
+        q = chunk(j)
+        return remote(sib_out.at[q], sib_in.at[q], sib_sem, (j,), sibling)
+
+    def grads(first_stage):
+        for j in (first_stage, first_stage + 1):
+            cot_copy(j).wait_recv()
+
+        def body(i, carry):
+            q = chunk(first_stage + i)
+            for tap in range(3):
+                total = jnp.zeros((rows, width), F32)
+                for b in range(seqs):
+                    at = slice(tap * DILATION_STEP, tap * DILATION_STEP + span)
+                    near_row = fs * outs + q * rows
+                    columns = slice(b * span, (b + 1) * span)
+                    total += jnp.dot(
+                        cot[pl.ds(near_row, rows), columns],
+                        hidden[b, at, :],
+                        preferred_element_type=F32,
+                    )
+                    total += jnp.dot(
+                        far_cot[pl.ds(q * rows, rows), columns],
+                        far_hidden[b, at, :],
+                        preferred_element_type=F32,
+                    )
+                total = total * scale
+                low, high = total[:mine], total[mine:]
+                own[q, tap] = jnp.where(core == 0, low, high)
+                sib_out[q, tap] = jnp.where(core == 0, high, low).astype(BF16)
+            return carry
+
+        lax.fori_loop(0, 2, body, 0)
+        for j in (first_stage, first_stage + 1):
+            sib_copy(j).start()
+        for j in (first_stage, first_stage + 1):
+            sib_copy(j).wait_recv()
+            q = chunk(j)
+            for tap in range(3):
+                own[q, tap] += sib_in[q, tap].astype(F32)
+
+    def columns(d):
+        return slice(d * half, (d + 1) * half)
+
+    def behind(d, count):
+        return (p + (ring - count if d == 0 else count)) % ring
+
+    grads(0)
+    for d in range(2):
+        for tap in range(3):
+            first[d, tap] = own[behind(d, 1), tap, :, columns(d)].astype(BF16)
+
+    def part_copy(d, s):
+        source = first.at[d] if s == 0 else part.at[d, s - 1]
+        return remote(source, part.at[d, s], part_sem, (d, s), (right, left)[d])
+
+    mix_copy = remote(mix_out, mix_in, mix_sem, (0,), far)
+    for s in range(ring - 1):
+        for d in range(2):
+            part_copy(d, s).start()
+        if 2 * s + 2 < ring:
+            grads(2 * s + 2)
+        elif 2 * s == ring:
+            forward(far_hidden, emit_far)
+            mix_copy.start()
+        for d in range(2):
+            part_copy(d, s).wait_recv()
+            if s < ring - 2:
+                q = behind(d, s + 2)
+                for tap in range(3):
+                    value = part[d, s, tap].astype(F32) + own[q, tap, :, columns(d)]
+                    part[d, s, tap] = value.astype(BF16)
+
+    noise_load.wait()
+    for d in range(2):
+        for tap in range(3):
+            at = columns(d)
+            grad = part[d, ring - 2, tap].astype(F32) + own[p, tap, :, at]
+            fresh[tap, :, at] = (
+                param[tap, pl.ds(own_rows, mine), at].astype(F32)
+                - eta * grad
+                + math.sqrt(2.0 * eta) * noise[tap, :, at].astype(F32)
+            ).astype(BF16)
+
+    def place(q, at):
+        return new_param.at[:, pl.ds(q * rows + core * mine, mine), at]
+
+    def gather_copy(d, s):
+        spot = place(behind(d, s) if s else p, columns(d))
+        source = fresh.at[:, :, columns(d)] if s == 0 else spot
+        return remote(source, spot, gather_sem, (d, s), (right, left)[d])
+
+    def share_copy(d, s):
+        spot = place(behind(d, s) if s else p, columns(d))
+        source = fresh.at[:, :, columns(d)] if s == 0 else spot
+        return remote(source, spot, share_sem, (d, s), sibling)
+
+    keep = pltpu.make_async_copy(fresh, place(p, slice(0, width)), load_sem.at[2])
+    for d in range(2):
+        gather_copy(d, 0).start()
+    keep.start()
+    for d in range(2):
+        share_copy(d, 0).start()
+    for s in range(ring - 1):
+        if s == ring - 2:
+            mix_copy.wait_recv()
+            at = pl.ds(pl.multiple_of((1 - fs) * outs, 128), outs)
+            for b in range(seqs):
+                outputs[b, :, at] = (
+                    inputs[b, :, at].astype(F32) + mix_in[b].astype(F32)
+                ).astype(BF16)
+        for d in range(2):
+            gather_copy(d, s).wait_recv()
+            if s < ring - 2:
+                gather_copy(d, s + 1).start()
+            share_copy(d, s + 1).start()
+
+    for d in range(2):
+        for s in range(ring):
+            share_copy(d, s).wait()
+        for s in range(ring - 1):
+            gather_copy(d, s).wait_send()
+            part_copy(d, s).wait_send()
+    for j in range(ring):
+        cot_copy(j).wait_send()
+        sib_copy(j).wait_send()
+    hid_copy.wait_send()
+    mix_copy.wait_send()
+    keep.wait()
+
+
+def ring_step(inputs, gain, param, cotangent, noise):
+    seqs, span, width = inputs.shape
+    outs = param.shape[0]
+    ring = lax.axis_size("seq") // 2
+    scale = 1.0 / math.sqrt(3.0 * width)
+    total_rows = seqs * lax.axis_size("fsdp") * span * lax.axis_size("seq")
+    eta = math.sqrt(3.0 * width / total_rows)
+    hidden = padded(normalise(inputs, gain), (("seq", 1),), DILATION_STEP)
+    cot = jnp.transpose(cotangent, (2, 0, 1)).reshape(width, seqs * span)
+    mine = outs // ring // 2
+    vmem, anywhere = (pl.BlockSpec(memory_space=pltpu.VMEM), pl.BlockSpec(memory_space=pl.ANY))
+    dma = pltpu.SemaphoreType.DMA
+    flops = 4 * 3 * 2 * seqs * span * width * outs
+    outputs, new_param = pl.pallas_call(
+        functools.partial(ring_kernel, ring, scale, eta),
+        out_shape=(
+            jax.ShapeDtypeStruct(inputs.shape, BF16),
+            jax.ShapeDtypeStruct((3, outs, width), BF16),
+        ),
+        in_specs=[vmem, vmem, vmem, anywhere, anywhere],
+        out_specs=(vmem, anywhere),
+        scratch_shapes=[
+            pltpu.VMEM((3, outs, width), BF16),
+            pltpu.VMEM((3, mine, width), BF16),
+            pltpu.VMEM(hidden.shape, BF16),
+            pltpu.VMEM((outs, seqs * span), BF16),
+            pltpu.VMEM((ring, 3, mine, width), F32),
+            pltpu.VMEM((ring, 3, mine, width), BF16),
+            pltpu.VMEM((ring, 3, mine, width), BF16),
+            pltpu.VMEM((2, 3, mine, width // 2), BF16),
+            pltpu.VMEM((2, ring - 1, 3, mine, width // 2), BF16),
+            pltpu.VMEM((3, mine, width), BF16),
+            pltpu.VMEM((seqs, span, outs), BF16),
+            pltpu.VMEM((seqs, span, outs), BF16),
+            dma((3,)),
+            dma((2, 1)),
+            dma((2, ring)),
+            dma((2, ring)),
+            dma((2, 2, ring - 1)),
+            dma((2, 2, ring - 1)),
+            dma((2, 2, ring)),
+            dma((2, 1)),
+        ],
+        compiler_params=pltpu.CompilerParams(
+            collective_id=0, has_side_effects=True, vmem_limit_bytes=60 * 2**20
+        ),
+        cost_estimate=pl.CostEstimate(
+            flops=flops, bytes_accessed=30 * 2**20, transcendentals=0
+        ),
+    )(
+        hidden,
+        cot,
+        inputs,
+        jnp.transpose(param, (1, 0, 2)),
+        jnp.transpose(noise, (1, 0, 2)),
+    )
+    return (outputs, jnp.transpose(new_param, (1, 0, 2)))
+
+
+def fits(mesh):
+    seq, fsdp = mesh.shape["seq"], mesh.shape["fsdp"]
+
+    def step(inputs, gain, param, cotangent, noise):
+        seqs, span, width = inputs.shape
+        outs = param.shape[0]
+        ok = fsdp == 2 and seq % 8 == 0 and outs % (16 * seq) == 0
+        ok = ok and span % 128 == 0 and width % 256 == 0 and outs % 256 == 0
+        return (ring_step if ok else shards)(inputs, gain, param, cotangent, noise)
+
+    return step
+
+
 def solution(mesh):
     placed = (
         P("fsdp", "seq", None),
@@ -93,7 +427,7 @@
         P("fsdp", None, None),
     )
     return jax.shard_map(
-        shards,
+        fits(mesh),
         mesh=mesh,
         in_specs=placed,
         out_specs=(P("fsdp", "seq", None), P("fsdp", None, None)),

time: 797 us -> 172 us (0.22)
  waiting for transfers between devices: 717 us -> 2.44 us
  Pallas kernels: 0 us -> 149 us
  matrix products: 19.1 us -> 0 us
  local copies, waits for them, and re-layouts: 27.5 us -> 10.7 us
  between operations: 14.5 us -> 0.69 us
  other arithmetic: 14.3 us -> 6.02 us
    unnamed x5 -> x0, waiting for transfers between devices: 328 us -> none
    all_gather x2 -> x0, waiting for transfers between devices: 224 us -> none  [the longest x1 167 us: shards(): lax.all_gather(param, 'fsdp', axis=0, tiled=True)]
    reduce_scatter x1 -> x0, waiting for transfers between devices: 165 us -> none  [shards(): lax.psum_scatter(term.astype(jnp.float32).astype(jnp.bfloat16), 'fsdp', s...]
    pallas_call x0 -> x1, Pallas kernels: none -> 149 us  [ring_step(): pl.pallas_call(functools.partial(ring_kernel, ring, scale, eta), out_shap...]
    dot_general x6 -> x0, matrix products: 19.1 us -> none  [the longest x3 11.2 us: convolve(): lax.dot_general(input_window, kernel[:, kernel_tap, :], (((2,), (1,)), ((...]
    convert_element_type x1 -> x0, local copies, waits for them, and re-layouts: 17.1 us -> none  [shards(): share = lax.psum_scatter(term.astype(jnp.float32).astype(jnp.bfloat16), '...]
    convert_element_type x2 -> x0, other arithmetic: 9.64 us -> none  [the longest x1 7.33 us: shards(): term = (jnp.stack(taps, axis=1) * scale).astype(jnp.bfloat16)]
  transfers between devices with their start and end apart: 6 -> 2, of which waited for: 4 -> 1; matrix products, arithmetic and copies ran while one was open for 3% -> 1% of each run, Pallas kernels for 0% -> 0%
where the time goes in v1:
time: 172 us
  Pallas kernels  149 us (87%)
  local copies, waits for them, and re-layouts  10.7 us (6%)
  other arithmetic  6.02 us (4%)
  starting transfers between devices  3.65 us (2%)
  waiting for transfers between devices  2.44 us (1%)
    pallas_call x1, Pallas kernels, ring_step(): pl.pallas_call(functools.partial(ring_kernel, ring, scale, eta), out_shap...  149 us
    unnamed x4, local copies, waits for them, and re-layouts  9.08 us
  transfers between devices with their start and end apart: 2, of which 1 were waited for; matrix products, arithmetic and copies ran while one was open for 1% of the time, Pallas kernels for 0%

profile of v1, /device:TPU:0, one launch (start us, length us, event | category | flops | bytes accessed | tf_op | source)
XLA Modules:
  0.0 172.2 jit_solution(12781225074224922517)
XLA Ops:
  0.6 0.0 copy-start
  0.6 1.9 %fusion = f32[2,256]{1,0:T(2,128)S(1)} fusion(bf16[2,256,1536]{2,1,0:T(8,128)(2,1)} %inputs.1), kind=kLoop, calls=%fused_computation.3 | loop fusion | flops 2358784 | bytes 1574912 | tf_op jit(solution)/shard_map/reduce_sum | solution.py:32
  2.6 2.8 %fusion.4 = bf16[2,256,1536]{2,1,0:T(8,128)(2,1)S(1)} fusion(bf16[2,256,1536]{2,1,0:T(8,128)(2,1)} %inputs.1, f32[1536]{0:T(1024)} %param.6, f32[2,256]{1,0:T(2,128)S(1)} %add_rsqrt_fusion), kind=kLoop, calls=%fused_computation.7 | loop fusion | flops 9437184 | bytes 3153920 | tf_op jit(solution)/shard_map/convert_element_type | solution.py:33
  5.4 2.4 %collective-permute-start = (bf16[2,16,1536]{2,1,0:T(8,128)(2,1)S(1)}, bf16[2,16,1536]{2,1,0:T(8,128)(2,1)S(1)}, u32[]{:S(2)}, u32[]{:S(2)}) collective-permute-start(bf16[2,16,1536]{2,1,0:T(8,128)(2,1)S(1)} %get-tuple-element.6), channel_id=1, source_target_pairs={{0,2},{2,4},{4,6},{6,8},{8,10},{10,12},{12,14},{14,16},{16,18},{18... | collective-permute-start | bytes 294920 | tf_op jit(solution)/shard_map/ppermute | solution.py:24
  7.7 1.3 collective-permute-start.1
  9.0 0.0 copy-done
  9.1 1.6 copy.8.cot
  10.6 0.0 collective-permute-done
  10.6 2.4 %collective-permute-done.1 = bf16[2,16,1536]{2,1,0:T(8,128)(2,1)S(1)} collective-permute-done((bf16[2,16,1536]{2,1,0:T(8,128)(2,1)S(1)}, bf16[2,16,1536]{2,1,0:T(8,128)(2,1)S(1)}, u32[]{:S(2)}, u32[]{:S(2)}) %collective-permute-start.1) | collective-permute-done | bytes 98336 | tf_op jit(solution)/shard_map/ppermute | solution.py:25
  13.1 1.3 pad_maximum_fusion.hidden
  14.4 148.8 %shard_map.68 = (bf16[2,256,1536]{2,1,0:T(8,128)(2,1)}, bf16[3,768,1536]{2,1,0:T(8,128)(2,1)}) custom-call(bf16[2,288,1536]{2,1,0:T(8,128)(2,1)} %pad_maximum_fusion.hidden, bf16[1536,512]{1,0:T(8,128)(2,1)} %copy.8.cot, bf16[2,256,1536]{2,1,0:T(8,128)(2,1)} %inputs.1, bf16[3,768,1536]{2,1,0:T(8,128)(2,1)} %bitcast.8, bf16[3,768,1536]{2,1,0:T(8,128)(2,1)} %bitcast.9), custom_call_target="tpu_custom_call" | custom-call | flops 14495514624 | bytes 31457280 | tf_op jit(solution)/shard_map/pallas_call | solution.py:362
  163.2 2.7 %copy.11 = bf16[2,256,1536]{2,1,0:T(8,128)(2,1)} copy(bf16[2,256,1536]{2,1,0:T(8,128)(2,1)} %get-tuple-element.10) | data formatting | bytes 3145728
  165.8 6.4 %copy.12 = bf16[768,3,1536]{2,0,1:T(8,128)(2,1)} copy(bf16[768,3,1536]{2,0,1:T(8,128)(2,1)} %bitcast.6) | data formatting | bytes 14155776
  (2 shorter events, 0.0 us)
Async XLA Ops:
  0.6 8.4 %copy-start = (bf16[2,256,1536]{2,1,0:T(8,128)(2,1)S(1)}, bf16[2,256,1536]{2,1,0:T(8,128)(2,1)}, u32[]{:S(2)}) copy-start(bf16[2,256,1536]{2,1,0:T(8,128)(2,1)} %param.8) | copy-start | bytes 4718596
  5.4 5.3 %collective-permute-start = (bf16[2,16,1536]{2,1,0:T(8,128)(2,1)S(1)}, bf16[2,16,1536]{2,1,0:T(8,128)(2,1)S(1)}, u32[]{:S(2)}, u32[]{:S(2)}) collective-permute-start(bf16[2,16,1536]{2,1,0:T(8,128)(2,1)S(1)} %get-tuple-element.6), channel_id=1, source_target_pairs={{0,2},{2,4},{4,6},{6,8},{8,10},{10,12},{12,14},{14,16},{16,18},{18... | collective-permute-start | bytes 294920 | tf_op jit(solution)/shard_map/ppermute | solution.py:24
  7.7 5.3 %collective-permute-start.1 = (bf16[2,16,1536]{2,1,0:T(8,128)(2,1)S(1)}, bf16[2,16,1536]{2,1,0:T(8,128)(2,1)S(1)}, u32[]{:S(2)}, u32[]{:S(2)}) collective-permute-start(bf16[2,16,1536]{2,1,0:T(8,128)(2,1)S(1)} %get-tuple-element.7), channel_id=1, source_target_pairs={{2,0},{4,2},{6,4},{8,6},{10,8},{12,10},{14,12},{16,14},{18,16},{20... | collective-permute-start | bytes 294920 | tf_op jit(solution)/shard_map/ppermute | solution.py:25

commit v2 on v1

--- a/solution.py
+++ b/solution.py
@@ -105,7 +105,7 @@
     noise,
     far_hidden,
     far_cot,
-    own,
+    near,
     sib_out,
     sib_in,
     first,
@@ -185,10 +185,10 @@
     for j in range(ring):
         cot_copy(j).start()
 
-    def forward(source, emit):
-        tile = 256
-        tiles = outs // tile
-
+    tile = 256
+    tiles = outs // tile
+
+    def forward(source, emit, start, stop):
         def body(i, carry):
             b, o = i // tiles, pl.multiple_of((i % tiles) * tile, tile)
             total = jnp.zeros((span, tile), F32)
@@ -202,7 +202,7 @@
             emit(b, o, tile, total * scale)
             return carry
 
-        lax.fori_loop(0, seqs * tiles, body, 0)
+        lax.fori_loop(start, stop, body, 0)
 
     def emit_near(b, o, tile, value):
         at = pl.ds(pl.multiple_of(fs * outs + o, 128), tile)
@@ -211,8 +211,25 @@
     def emit_far(b, o, tile, value):
         mix_out[b, :, pl.ds(o, tile)] = value.astype(BF16)
 
+    def window(tap):
+        return slice(tap * DILATION_STEP, tap * DILATION_STEP + span)
+
+    def near_grads(i, carry):
+        o = pl.multiple_of(i * tile, tile)
+        for tap in range(3):
+            total = jnp.zeros((tile, width), F32)
+            for b in range(seqs):
+                total += jnp.dot(
+                    cot[pl.ds(fs * outs + o, tile), b * span : (b + 1) * span],
+                    hidden[b, window(tap), :],
+                    preferred_element_type=F32,
+                )
+            near[tap, pl.ds(o, tile), :] = total * scale
+        return carry
+
+    lax.fori_loop(0, tiles, near_grads, 0)
     param_load.wait()
-    forward(hidden, emit_near)
+    forward(hidden, emit_near, 0, seqs * tiles)
     hid_copy.wait_recv()
 
     def sib_copy(j):
@@ -220,41 +237,24 @@
         return remote(sib_out.at[q], sib_in.at[q], sib_sem, (j,), sibling)
 
     def grads(first_stage):
-        for j in (first_stage, first_stage + 1):
+        for i in range(2):
+            j = first_stage + i
             cot_copy(j).wait_recv()
-
-        def body(i, carry):
-            q = chunk(first_stage + i)
+            q = chunk(j)
+            chunk_rows = pl.ds(q * rows, rows)
             for tap in range(3):
                 total = jnp.zeros((rows, width), F32)
                 for b in range(seqs):
-                    at = slice(tap * DILATION_STEP, tap * DILATION_STEP + span)
-                    near_row = fs * outs + q * rows
-                    columns = slice(b * span, (b + 1) * span)
                     total += jnp.dot(
-                        cot[pl.ds(near_row, rows), columns],
-                        hidden[b, at, :],
+                        far_cot[chunk_rows, b * span : (b + 1) * span],
+                        far_hidden[b, window(tap), :],
                         preferred_element_type=F32,
                     )
-                    total += jnp.dot(
-                        far_cot[pl.ds(q * rows, rows), columns],
-                        far_hidden[b, at, :],
-                        preferred_element_type=F32,
-                    )
-                total = total * scale
+                total = total * scale + near[tap, chunk_rows, :]
+                near[tap, chunk_rows, :] = total
                 low, high = total[:mine], total[mine:]
-                own[q, tap] = jnp.where(core == 0, low, high)
                 sib_out[q, tap] = jnp.where(core == 0, high, low).astype(BF16)
-            return carry
-
-        lax.fori_loop(0, 2, body, 0)
-        for j in (first_stage, first_stage + 1):
             sib_copy(j).start()
-        for j in (first_stage, first_stage + 1):
-            sib_copy(j).wait_recv()
-            q = chunk(j)
-            for tap in range(3):
-                own[q, tap] += sib_in[q, tap].astype(F32)
 
     def columns(d):
         return slice(d * half, (d + 1) * half)
@@ -262,82 +262,100 @@
     def behind(d, count):
         return (p + (ring - count if d == 0 else count)) % ring
 
-    grads(0)
-    for d in range(2):
-        for tap in range(3):
-            first[d, tap] = own[behind(d, 1), tap, :, columns(d)].astype(BF16)
-
-    def part_copy(d, s):
-        source = first.at[d] if s == 0 else part.at[d, s - 1]
-        return remote(source, part.at[d, s], part_sem, (d, s), (right, left)[d])
-
-    mix_copy = remote(mix_out, mix_in, mix_sem, (0,), far)
-    for s in range(ring - 1):
-        for d in range(2):
-            part_copy(d, s).start()
-        if 2 * s + 2 < ring:
-            grads(2 * s + 2)
-        elif 2 * s == ring:
-            forward(far_hidden, emit_far)
-            mix_copy.start()
-        for d in range(2):
-            part_copy(d, s).wait_recv()
-            if s < ring - 2:
-                q = behind(d, s + 2)
-                for tap in range(3):
-                    value = part[d, s, tap].astype(F32) + own[q, tap, :, columns(d)]
-                    part[d, s, tap] = value.astype(BF16)
-
-    noise_load.wait()
-    for d in range(2):
-        for tap in range(3):
-            at = columns(d)
-            grad = part[d, ring - 2, tap].astype(F32) + own[p, tap, :, at]
-            fresh[tap, :, at] = (
-                param[tap, pl.ds(own_rows, mine), at].astype(F32)
-                - eta * grad
-                + math.sqrt(2.0 * eta) * noise[tap, :, at].astype(F32)
-            ).astype(BF16)
-
-    def place(q, at):
-        return new_param.at[:, pl.ds(q * rows + core * mine, mine), at]
-
-    def gather_copy(d, s):
-        spot = place(behind(d, s) if s else p, columns(d))
-        source = fresh.at[:, :, columns(d)] if s == 0 else spot
-        return remote(source, spot, gather_sem, (d, s), (right, left)[d])
+    def own(q, tap, d):
+        at = near[tap, pl.ds(q * rows + core * mine, mine), columns(d)]
+        return at + sib_in[q, tap, :, columns(d)].astype(F32)
+
+    def part_copy(d, s, tap):
+        source = first.at[d, tap] if s == 0 else part.at[d, s - 1, tap]
+        to = (right, left)[d]
+        return remote(source, part.at[d, s, tap], part_sem, (d, s, tap), to)
+
+    def place(q, tap, at):
+        return new_param.at[tap, pl.ds(q * rows + core * mine, mine), at]
+
+    def gather_copy(d, s, tap):
+        spot = place(behind(d, s), tap, columns(d))
+        source = fresh.at[tap, :, columns(d)] if s == 0 else spot
+        return remote(source, spot, gather_sem, (d, s, tap), (right, left)[d])
 
     def share_copy(d, s):
-        spot = place(behind(d, s) if s else p, columns(d))
+        q = behind(d, s)
+        spot = new_param.at[:, pl.ds(q * rows + core * mine, mine), columns(d)]
         source = fresh.at[:, :, columns(d)] if s == 0 else spot
         return remote(source, spot, share_sem, (d, s), sibling)
 
-    keep = pltpu.make_async_copy(fresh, place(p, slice(0, width)), load_sem.at[2])
-    for d in range(2):
-        gather_copy(d, 0).start()
+    grads(0)
+    for j in range(2):
+        sib_copy(j).wait_recv()
+    for tap in range(3):
+        for d in range(2):
+            first[d, tap] = own(behind(d, 1), tap, d).astype(BF16)
+            part_copy(d, 0, tap).start()
+
+    mix_copy = remote(mix_out, mix_in, mix_sem, (0,), far)
+    stages = ring // 2 - 1
+    spread = ring - 2 - stages
+    pieces = seqs * tiles
+    for s in range(ring - 1):
+        if s < stages:
+            grads(2 * s + 2)
+            for j in range(2):
+                sib_copy(2 * s + 2 + j).wait_recv()
+        elif s < ring - 2:
+            at = s - stages
+            forward(
+                far_hidden, emit_far, at * pieces // spread, (at + 1) * pieces // spread
+            )
+            if at == spread - 1:
+                mix_copy.start()
+        else:
+            noise_load.wait()
+        for tap in range(3):
+            for d in range(2):
+                part_copy(d, s, tap).wait_recv()
+                total = part[d, s, tap].astype(F32) + own(behind(d, s + 2), tap, d)
+                if s < ring - 2:
+                    part[d, s, tap] = total.astype(BF16)
+                    part_copy(d, s + 1, tap).start()
+                else:
+                    at = columns(d)
+                    fresh[tap, :, at] = (
+                        param[tap, pl.ds(own_rows, mine), at].astype(F32)
+                        - eta * total
+                        + math.sqrt(2.0 * eta) * noise[tap, :, at].astype(F32)
+                    ).astype(BF16)
+                    gather_copy(d, 0, tap).start()
+
+    keep = pltpu.make_async_copy(
+        fresh, new_param.at[:, pl.ds(own_rows, mine), :], load_sem.at[2]
+    )
     keep.start()
     for d in range(2):
         share_copy(d, 0).start()
     for s in range(ring - 1):
-        if s == ring - 2:
+        if s == ring - 3:
             mix_copy.wait_recv()
             at = pl.ds(pl.multiple_of((1 - fs) * outs, 128), outs)
             for b in range(seqs):
                 outputs[b, :, at] = (
                     inputs[b, :, at].astype(F32) + mix_in[b].astype(F32)
                 ).astype(BF16)
+        for tap in range(3):
+            for d in range(2):
+                gather_copy(d, s, tap).wait_recv()
+                if s < ring - 2:
+                    gather_copy(d, s + 1, tap).start()
         for d in range(2):
-            gather_copy(d, s).wait_recv()
-            if s < ring - 2:
-                gather_copy(d, s + 1).start()
             share_copy(d, s + 1).start()
 
     for d in range(2):
         for s in range(ring):
             share_copy(d, s).wait()
         for s in range(ring - 1):
-            gather_copy(d, s).wait_send()
-            part_copy(d, s).wait_send()
+            for tap in range(3):
+                gather_copy(d, s, tap).wait_send()
+                part_copy(d, s, tap).wait_send()
     for j in range(ring):
         cot_copy(j).wait_send()
         sib_copy(j).wait_send()
@@ -372,7 +390,7 @@
             pltpu.VMEM((3, mine, width), BF16),
             pltpu.VMEM(hidden.shape, BF16),
             pltpu.VMEM((outs, seqs * span), BF16),
-            pltpu.VMEM((ring, 3, mine, width), F32),
+            pltpu.VMEM((3, outs, width), F32),
             pltpu.VMEM((ring, 3, mine, width), BF16),
             pltpu.VMEM((ring, 3, mine, width), BF16),
             pltpu.VMEM((2, 3, mine, width // 2), BF16),
@@ -384,13 +402,13 @@
             dma((2, 1)),
             dma((2, ring)),
             dma((2, ring)),
-            dma((2, 2, ring - 1)),
-            dma((2, 2, ring - 1)),
+            dma((2, 2, ring - 1, 3)),
+            dma((2, 2, ring - 1, 3)),
             dma((2, 2, ring)),
             dma((2, 1)),
         ],
         compiler_params=pltpu.CompilerParams(
-            collective_id=0, has_side_effects=True, vmem_limit_bytes=60 * 2**20
+            collective_id=0, has_side_effects=True, vmem_limit_bytes=50 * 2**20
         ),
         cost_estimate=pl.CostEstimate(
             flops=flops, bytes_accessed=30 * 2**20, transcendentals=0

time: 172 us -> 150 us (0.87)
  Pallas kernels: 149 us -> 128 us
    pallas_call x1, Pallas kernels: 149 us -> 128 us  [ring_step(): pl.pallas_call(functools.partial(ring_kernel, ring, scale, eta), out_shap...]
    unnamed x4 -> x2, local copies, waits for them, and re-layouts: 9.08 us -> 7.57 us
where the time goes in v2:
time: 150 us
  Pallas kernels  128 us (85%)
  local copies, waits for them, and re-layouts  9.3 us (6%)
  other arithmetic  5.9 us (4%)
  starting transfers between devices  3.65 us (2%)
  waiting for transfers between devices  2.29 us (2%)
    pallas_call x1, Pallas kernels, ring_step(): pl.pallas_call(functools.partial(ring_kernel, ring, scale, eta), out_shap...  128 us
    unnamed x2, local copies, waits for them, and re-layouts  7.57 us
  transfers between devices with their start and end apart: 2, of which 1 were waited for; matrix products, arithmetic and copies ran while one was open for 1% of the time, Pallas kernels for 0%

profile of v2, /device:TPU:0, one launch (start us, length us, event | category | flops | bytes accessed | tf_op | source)
XLA Modules:
  0.0 149.9 jit_solution(336860050947504669)
XLA Ops:
  0.6 1.8 %fusion = f32[2,256]{1,0:T(2,128)S(1)} fusion(bf16[2,256,1536]{2,1,0:T(8,128)(2,1)} %inputs.1), kind=kLoop, calls=%fused_computation.3 | loop fusion | flops 2358784 | bytes 1574912 | tf_op jit(solution)/shard_map/reduce_sum | solution.py:32
  2.4 2.8 %fusion.4 = bf16[2,256,1536]{2,1,0:T(8,128)(2,1)S(1)} fusion(bf16[2,256,1536]{2,1,0:T(8,128)(2,1)} %inputs.1, f32[1536]{0:T(1024)} %param.6, f32[2,256]{1,0:T(2,128)S(1)} %add_rsqrt_fusion), kind=kLoop, calls=%fused_computation.7 | loop fusion | flops 9437184 | bytes 3153920 | tf_op jit(solution)/shard_map/convert_element_type | solution.py:33
  5.2 2.4 %collective-permute-start = (bf16[2,16,1536]{2,1,0:T(8,128)(2,1)S(1)}, bf16[2,16,1536]{2,1,0:T(8,128)(2,1)S(1)}, u32[]{:S(2)}, u32[]{:S(2)}) collective-permute-start(bf16[2,16,1536]{2,1,0:T(8,128)(2,1)S(1)} %get-tuple-element.6), channel_id=1, source_target_pairs={{0,2},{2,4},{4,6},{6,8},{8,10},{10,12},{12,14},{14,16},{16,18},{18... | collective-permute-start | bytes 294920 | tf_op jit(solution)/shard_map/ppermute | solution.py:24
  7.6 1.3 collective-permute-start.1
  8.9 1.7 %copy.8.cot = bf16[1536,512]{1,0:T(8,128)(2,1)S(1)} copy(bf16[1536,512]{0,1:T(8,128)(2,1)} %bitcast.7) | data formatting | bytes 3145728 | tf_op jit(solution)/shard_map/reshape | solution.py:375
  10.6 0.0 collective-permute-done
  10.7 2.3 %collective-permute-done.1 = bf16[2,16,1536]{2,1,0:T(8,128)(2,1)S(1)} collective-permute-done((bf16[2,16,1536]{2,1,0:T(8,128)(2,1)S(1)}, bf16[2,16,1536]{2,1,0:T(8,128)(2,1)S(1)}, u32[]{:S(2)}, u32[]{:S(2)}) %collective-permute-start.1) | collective-permute-done | bytes 98336 | tf_op jit(solution)/shard_map/ppermute | solution.py:25
  12.9 1.3 pad_maximum_fusion.hidden
  14.3 128.0 %shard_map.68 = (bf16[2,256,1536]{2,1,0:T(8,128)(2,1)S(1)}, bf16[3,768,1536]{2,1,0:T(8,128)(2,1)}) custom-call(bf16[2,288,1536]{2,1,0:T(8,128)(2,1)} %pad_maximum_fusion.hidden, bf16[1536,512]{1,0:T(8,128)(2,1)S(1)} %copy.8.cot, bf16[2,256,1536]{2,1,0:T(8,128)(2,1)} %inputs.1, bf16[3,768,1536]{2,1,0:T(8,128)(2,1)} %bitcast.8, bf16[3,768,1536]{2,1,0:T(8,128)(2,1)} %bitcast.9), custom_call_target="tpu_custom_call" | custom-call | flops 14495514624 | bytes 31457280 | tf_op jit(solution)/shard_map/pallas_call | solution.py:380
  142.3 1.1 copy.11
  143.5 6.4 %copy.12 = bf16[768,3,1536]{2,0,1:T(8,128)(2,1)} copy(bf16[768,3,1536]{2,0,1:T(8,128)(2,1)} %bitcast.6) | data formatting | bytes 14155776
  (2 shorter events, 0.0 us)
Async XLA Ops:
  5.2 5.4 %collective-permute-start = (bf16[2,16,1536]{2,1,0:T(8,128)(2,1)S(1)}, bf16[2,16,1536]{2,1,0:T(8,128)(2,1)S(1)}, u32[]{:S(2)}, u32[]{:S(2)}) collective-permute-start(bf16[2,16,1536]{2,1,0:T(8,128)(2,1)S(1)} %get-tuple-element.6), channel_id=1, source_target_pairs={{0,2},{2,4},{4,6},{6,8},{8,10},{10,12},{12,14},{14,16},{16,18},{18... | collective-permute-start | bytes 294920 | tf_op jit(solution)/shard_map/ppermute | solution.py:24
  7.6 5.3 %collective-permute-start.1 = (bf16[2,16,1536]{2,1,0:T(8,128)(2,1)S(1)}, bf16[2,16,1536]{2,1,0:T(8,128)(2,1)S(1)}, u32[]{:S(2)}, u32[]{:S(2)}) collective-permute-start(bf16[2,16,1536]{2,1,0:T(8,128)(2,1)S(1)} %get-tuple-element.7), channel_id=1, source_target_pairs={{2,0},{4,2},{6,4},{8,6},{10,8},{12,10},{14,12},{16,14},{18,16},{20... | collective-permute-start | bytes 294920 | tf_op jit(solution)/shard_map/ppermute | solution.py:25

commit v3 on v2

--- a/solution.py
+++ b/solution.py
@@ -94,7 +94,7 @@
     ring,
     scale,
     eta,
-    hidden,
+    body_hidden,
     cot,
     inputs,
     param_hbm,
@@ -103,6 +103,7 @@
     new_param,
     param,
     noise,
+    hidden,
     far_hidden,
     far_cot,
     near,
@@ -114,6 +115,7 @@
     mix_out,
     mix_in,
     load_sem,
+    edge_sem,
     hid_sem,
     cot_sem,
     sib_sem,
@@ -150,9 +152,18 @@
     noise_load.start()
 
     barrier = pltpu.get_barrier_semaphore()
-    for other in (right, left, sibling, far):
+    for other in (right, left, far):
         pl.semaphore_signal(barrier, inc=1, device_id=other, device_id_type=MESH)
-    pl.semaphore_wait(barrier, 4)
+    has_before, has_after = seq > 0, seq < 2 * ring - 1
+    before, after = {"seq": seq - 1}, {"seq": seq + 1}
+    for there, other in ((has_before, before), (has_after, after)):
+
+        @pl.when(there)
+        def _():
+            pl.semaphore_signal(barrier, inc=1, device_id=other, device_id_type=MESH)
+
+    edges = jnp.where(has_before, 1, 0) + jnp.where(has_after, 1, 0)
+    pl.semaphore_wait(barrier, 3 + edges)
 
     def remote(src, dst, sems, index, to):
         return pltpu.make_async_remote_copy(
@@ -169,8 +180,26 @@
         offset = jnp.where(j % 2 == 0, ring - m, m)
         return (p + jnp.where(j == ring - 1, 0, offset)) % ring
 
-    hid_copy = remote(hidden, far_hidden, hid_sem, (0,), far)
+    step = DILATION_STEP
+    inner, head, tail = (slice(step, step + span), slice(0, step), slice(step + span, None))
+    edge_up = remote(
+        body_hidden.at[:, span - step :, :], hidden.at[:, head, :], edge_sem, (0,), after
+    )
+    edge_down = remote(
+        body_hidden.at[:, :step, :], hidden.at[:, tail, :], edge_sem, (1,), before
+    )
+    pl.when(has_after)(edge_up.start)
+    pl.when(has_before)(edge_down.start)
+    hid_copy = remote(body_hidden, far_hidden.at[:, inner, :], hid_sem, (0,), far)
     hid_copy.start()
+    inner_copy = pltpu.make_async_copy(body_hidden, hidden.at[:, inner, :], load_sem.at[3])
+    inner_copy.start()
+    for there, where in ((has_before, head), (has_after, tail)):
+
+        @pl.when(jnp.logical_not(there))
+        def _():
+            hidden[:, where, :] = jnp.zeros((seqs, step, width), BF16)
+
 
     def cot_copy(j):
         q = chunk(j)
@@ -227,10 +256,22 @@
             near[tap, pl.ds(o, tile), :] = total * scale
         return carry
 
+    edge_head = remote(
+        hidden.at[:, head, :], far_hidden.at[:, head, :], hid_sem, (1,), far
+    )
+    edge_tail = remote(
+        hidden.at[:, tail, :], far_hidden.at[:, tail, :], hid_sem, (2,), far
+    )
+    pl.when(has_before)(edge_up.wait_recv)
+    edge_head.start()
+    pl.when(has_after)(edge_down.wait_recv)
+    edge_tail.start()
+    inner_copy.wait()
     lax.fori_loop(0, tiles, near_grads, 0)
     param_load.wait()
     forward(hidden, emit_near, 0, seqs * tiles)
-    hid_copy.wait_recv()
+    for copy in (hid_copy, edge_head, edge_tail):
+        copy.wait_recv()
 
     def sib_copy(j):
         q = chunk(j)
@@ -359,9 +400,28 @@
     for j in range(ring):
         cot_copy(j).wait_send()
         sib_copy(j).wait_send()
-    hid_copy.wait_send()
+    for copy in (hid_copy, edge_head, edge_tail):
+        copy.wait_send()
+    pl.when(has_after)(edge_up.wait_send)
+    pl.when(has_before)(edge_down.wait_send)
     mix_copy.wait_send()
     keep.wait()
+
+
+def move_kernel(source, target, sems):
+    taps, outs, _ = source.shape
+    part = outs // 4
+    copies = []
+    for tap in range(taps):
+        for i in range(4):
+            at = (tap, slice(i * part, (i + 1) * part))
+            copies.append(
+                pltpu.make_async_copy(source.at[at], target.at[at], sems.at[tap, i])
+            )
+    for copy in copies:
+        copy.start()
+    for copy in copies:
+        copy.wait()
 
 
 def ring_step(inputs, gain, param, cotangent, noise):
@@ -371,7 +431,8 @@
     scale = 1.0 / math.sqrt(3.0 * width)
     total_rows = seqs * lax.axis_size("fsdp") * span * lax.axis_size("seq")
     eta = math.sqrt(3.0 * width / total_rows)
-    hidden = padded(normalise(inputs, gain), (("seq", 1),), DILATION_STEP)
+    hidden = normalise(inputs, gain)
+    wide = (seqs, span + 2 * DILATION_STEP, width)
     cot = jnp.transpose(cotangent, (2, 0, 1)).reshape(width, seqs * span)
     mine = outs // ring // 2
     vmem, anywhere = (pl.BlockSpec(memory_space=pltpu.VMEM), pl.BlockSpec(memory_space=pl.ANY))
@@ -388,7 +449,8 @@
         scratch_shapes=[
             pltpu.VMEM((3, outs, width), BF16),
             pltpu.VMEM((3, mine, width), BF16),
-            pltpu.VMEM(hidden.shape, BF16),
+            pltpu.VMEM(wide, BF16),
+            pltpu.VMEM(wide, BF16),
             pltpu.VMEM((outs, seqs * span), BF16),
             pltpu.VMEM((3, outs, width), F32),
             pltpu.VMEM((ring, 3, mine, width), BF16),
@@ -398,8 +460,9 @@
             pltpu.VMEM((3, mine, width), BF16),
             pltpu.VMEM((seqs, span, outs), BF16),
             pltpu.VMEM((seqs, span, outs), BF16),
-            dma((3,)),
-            dma((2, 1)),
+            dma((4,)),
+            dma((2, 2)),
+            dma((2, 3)),
             dma((2, ring)),
             dma((2, ring)),
             dma((2, 2, ring - 1, 3)),
@@ -420,6 +483,16 @@
         jnp.transpose(param, (1, 0, 2)),
         jnp.transpose(noise, (1, 0, 2)),
     )
+    new_param = pl.pallas_call(
+        move_kernel,
+        out_shape=jax.ShapeDtypeStruct(new_param.shape, BF16),
+        in_specs=[anywhere],
+        out_specs=anywhere,
+        scratch_shapes=[dma((3, 4))],
+        cost_estimate=pl.CostEstimate(
+            flops=0, bytes_accessed=2 * new_param.size * 2, transcendentals=0
+        ),
+    )(new_param)
     return (outputs, jnp.transpose(new_param, (1, 0, 2)))
 
 

time: 150 us -> 364 us (2.43)
  Pallas kernels: 128 us -> 355 us
  local copies, waits for them, and re-layouts: 9.3 us -> 2.73 us
  starting transfers between devices: 3.65 us -> 0 us
    pallas_call x0 -> x1, Pallas kernels: none -> 216 us  [ring_step(): pl.pallas_call(move_kernel, out_shape=jax.ShapeDtypeStruct(new_param.shap...]
    pallas_call x1, Pallas kernels: 128 us -> 140 us  [ring_step(): pl.pallas_call(functools.partial(ring_kernel, ring, scale, eta), out_shap...]
    unnamed x2 -> x3, local copies, waits for them, and re-layouts: 7.57 us -> 1.15 us
    ppermute x2 -> x0, starting transfers between devices: 3.65 us -> none  [the longest x1 2.36 us: padded(): before = lax.ppermute(last, axis, up)]
  transfers between devices with their start and end apart: 2 -> 0, of which waited for: 1 -> 0; matrix products, arithmetic and copies ran while one was open for 1% -> 0% of each run, Pallas kernels for 0% -> 0%
where the time goes in v3:
time: 364 us; the launch traced here: 363 us
  Pallas kernels  355 us (98%)
  other arithmetic  4.7 us (1%)
    pallas_call x1, Pallas kernels, ring_step(): pl.pallas_call(move_kernel, out_shape=jax.ShapeDtypeStruct(new_param.shap...  216 us
    pallas_call x1, Pallas kernels, ring_step(): pl.pallas_call(functools.partial(ring_kernel, ring, scale, eta), out_shap...  140 us

profile of v3, /device:TPU:0, one launch (start us, length us, event | category | flops | bytes accessed | tf_op | source)
XLA Modules:
  0.0 363.5 jit_solution(6005415903963009248)
XLA Ops:
  0.6 0.0 copy-start
  0.6 1.9 fusion
  2.6 2.8 fusion.4.body_hidden
  5.3 0.0 copy-done
  5.4 1.6 copy.8.cot
  6.9 139.7 %shard_map.68 = (bf16[2,256,1536]{2,1,0:T(8,128)(2,1)S(1)}, bf16[3,768,1536]{2,1,0:T(8,128)(2,1)}) custom-call(bf16[2,256,1536]{2,1,0:T(8,128)(2,1)S(1)} %fusion.4.body_hidden, bf16[1536,512]{1,0:T(8,128)(2,1)} %copy.8.cot, bf16[2,256,1536]{2,1,0:T(8,128)(2,1)} %inputs.1, bf16[3,768,1536]{2,1,0:T(8,128)(2,1)} %bitcast.8, bf16[3,768,1536]{2,1,0:T(8,128)(2,1)} %bitcast.9), custom_call_target="tpu_custom_call" | custom-call | flops 14495514624 | bytes 31457280 | tf_op jit(solution)/shard_map/pallas_call | solution.py:441
  146.7 215.6 %shard_map.69 = bf16[3,768,1536]{2,1,0:T(8,128)(2,1)} custom-call(bf16[3,768,1536]{2,1,0:T(8,128)(2,1)} %get-tuple-element.5.source), custom_call_target="tpu_custom_call" | custom-call | bytes 14155776 | tf_op jit(solution)/shard_map/pallas_call | solution.py:486
  362.3 1.1 copy.10
  (1 shorter events, 0.0 us)
Async XLA Ops:
  0.6 4.7 %copy-start = (bf16[2,256,1536]{2,1,0:T(8,128)(2,1)S(1)}, bf16[2,256,1536]{2,1,0:T(8,128)(2,1)}, u32[]{:S(2)}) copy-start(bf16[2,256,1536]{2,1,0:T(8,128)(2,1)} %param.8) | copy-start | bytes 4718596
